TPU v7x, 32 devices: a whole 2x2x4 slice. The times are simulated.
32 devices in a mesh: groups: 2 (over y), down: 4 (over z), cross: 2 (over x), depth: 2 (over core).
Axes of the slice: x: 2, y: 2, z: 4, core: 2. Of those that a mesh axis runs over, the one named last changes fastest.
Arguments:
- positions: float32 [3, 16, 4, 4, 128], P(None, ('groups', 'down'), 'cross', 'depth'), parts along dimension 1, may hold values from -0.5 to 0.5
- velocities: float32 [3, 16, 4, 4, 128], P(None, ('groups', 'down'), 'cross', 'depth'), parts along dimension 1, may hold values from -6 to 6
- sphere_radii: float32 [16, 4, 4, 128], P(('groups', 'down'), 'cross', 'depth'), parts along dimension 0, may hold values from 0.08 to 0.12
- counts: int32 [16, 4, 4], P(('groups', 'down'), 'cross', 'depth'), parts along dimension 0, may hold values from 32 to 128, as said below
- coefficients: float32 [48], replicated, may hold values from -0.6 to 0.6
Outputs:
- velocity_new: float32 [3, 16, 4, 4, 128], P(None, ('groups', 'down'), 'cross', 'depth'), parts along dimension 1
- contact_force: float32 [3, 16, 4, 4, 128], P(None, ('groups', 'down'), 'cross', 'depth'), parts along dimension 1
- residual_field: float32 [16, 4, 4], P(('groups', 'down'), 'cross', 'depth'), parts along dimension 0
- gram_matrix: float32 [96, 48], P('groups'), parts along dimension 0
- moment_vector: float32 [96], P('groups'), parts along dimension 0
There are 2 independent parts, one for each index of `groups`. A program takes and returns all parts, laid end to end along the dimension named above; an argument that names none is the same for every part. Nothing has to cross between parts.
Inputs may be any that keep to these rules, and one draw needn't show every extreme that they name: `counts`: slots 0 to count - 1 of a cell hold spheres, the rest are padding; every cell of the bottom depth layer holds 128.
All inputs are finite; a program needn't handle non-finite values.
Results may differ from a plain program's by a relative error of at most 0.0003.
Values sent between devices are 32-bit elements; how exact they have to be, the bound alone decides.
No kernel may reach another device: no remote copies, remote signals or barrier semaphores. Data moves between devices by JAX's collectives and lax.ppermute only.
A program may use at most 128 MiB of HBM per device.

v0:
```python
import jax
import jax.numpy as jnp
from jax import lax
from jax.sharding import PartitionSpec as P

STIFFNESS = 100.0
DAMPING = 20.0
TIME_STEP = 0.05
KERNEL_WIDTH = 0.4
KERNEL_NORM = 64.0
SOFTENING = 0.0001
RADIUS_REF = 0.1
MASS_SHIFT = 0.1
NEIGHBOURS = tuple(
    (
        (shift_x, shift_y, shift_z)
        for shift_x in (-1, 0, 1)
        for shift_y in (-1, 0, 1)
        for shift_z in (-1, 0, 1)
    )
)
PAIR_LIST = ((0, 0), (0, 1), (0, 2), (1, 1), (1, 2), (2, 2))


def with_halo(value, sides, width):
    for axis, dim in sides:
        peers, length = (lax.axis_size(axis), value.shape[dim])
        up = [(i, (i + 1) % peers) for i in range(peers)]
        down = [(j, i) for i, j in up]
        last = lax.slice_in_dim(value, length - width, length, axis=dim)
        first = lax.slice_in_dim(value, 0, width, axis=dim)
        before = lax.ppermute(last, axis, up)
        after = lax.ppermute(first, axis, down)
        value = jnp.concatenate([before, value, after], axis=dim)
    return value


def contact(extended):
    size_x = extended.shape[1] - 2
    size_y = extended.shape[2] - 2
    size_z = extended.shape[3] - 2
    slot_count = extended.shape[4]
    centre = extended[:, 1 : size_x + 1, 1 : size_y + 1, 1 : size_z + 1]
    self_mask = 1.0 - jnp.eye(slot_count, dtype=jnp.float32)
    totals = jnp.zeros((10,) + centre.shape[1:], jnp.float32)
    for shift_x, shift_y, shift_z in NEIGHBOURS:
        beside = extended[
            :,
            1 + shift_x : 1 + shift_x + size_x,
            1 + shift_y : 1 + shift_y + size_y,
            1 + shift_z : 1 + shift_z + size_z,
        ]
        places = jnp.stack([beside[0] + shift_x, beside[1] + shift_y, beside[2] + shift_z])
        branch = centre[0:3, ..., :, None] - places[..., None, :]
        relative = centre[3:6, ..., :, None] - beside[3:6, ..., None, :]
        squared = jnp.sum(branch * branch, axis=0)
        distance = jnp.sqrt(squared + SOFTENING)
        closing = -jnp.sum(relative * branch, axis=0) / distance
        correlation = jnp.maximum(centre[6][..., :, None] + beside[6][..., None, :] - distance, 0.0)
        weight = correlation * (STIFFNESS + DAMPING * closing) / distance
        weight = weight * centre[7][..., :, None] * beside[7][..., None, :]
        if shift_x == 0 and shift_y == 0 and (shift_z == 0):
            weight = weight * self_mask
        columns = jnp.stack(
            [
                jnp.ones_like(places[0]),
                places[0],
                places[1],
                places[2],
                places[0] * places[0],
                places[0] * places[1],
                places[0] * places[2],
                places[1] * places[1],
                places[1] * places[2],
                places[2] * places[2],
            ]
        )
        totals = totals + jnp.einsum(
            "xyzij,kxyzj->kxyzi", weight, columns, precision=lax.Precision.HIGHEST
        )
    centres = centre[0:3]
    force = jnp.stack([centres[axis_id] * totals[0] - totals[1 + axis_id] for axis_id in range(3)])
    stress = jnp.stack(
        [
            0.5
            * (
                centres[left_index] * centres[right_index] * totals[0]
                - centres[left_index] * totals[1 + right_index]
                - centres[right_index] * totals[1 + left_index]
                + totals[4 + pair_id]
            )
            for pair_id, (left_index, right_index) in enumerate(PAIR_LIST)
        ]
    )
    return (force, stress)


def coarse(extended, moments):
    size_x = extended.shape[1] - 2
    size_y = extended.shape[2] - 2
    size_z = extended.shape[3] - 2
    fields = jnp.zeros((moments.shape[0], size_x, size_y, size_z), jnp.float32)
    for shift_x, shift_y, shift_z in NEIGHBOURS:
        beside = extended[
            :,
            1 + shift_x : 1 + shift_x + size_x,
            1 + shift_y : 1 + shift_y + size_y,
            1 + shift_z : 1 + shift_z + size_z,
        ]
        beside_moment = moments[
            :,
            1 + shift_x : 1 + shift_x + size_x,
            1 + shift_y : 1 + shift_y + size_y,
            1 + shift_z : 1 + shift_z + size_z,
        ]
        squared = (
            (beside[0] + shift_x) ** 2 + (beside[1] + shift_y) ** 2 + (beside[2] + shift_z) ** 2
        )
        kernel = jnp.exp(-squared / (2.0 * KERNEL_WIDTH * KERNEL_WIDTH)) * beside[7] / KERNEL_NORM
        fields = fields + jnp.sum(kernel * beside_moment, axis=-1)
    return fields


def library(padded, stress):
    slopes = [
        (padded[:, 2:, 1:-1, 1:-1] - padded[:, :-2, 1:-1, 1:-1]) * 0.5,
        (padded[:, 1:-1, 2:, 1:-1] - padded[:, 1:-1, :-2, 1:-1]) * 0.5,
        (padded[:, 1:-1, 1:-1, 2:] - padded[:, 1:-1, 1:-1, :-2]) * 0.5,
    ]
    centre = padded[:, 1:-1, 1:-1, 1:-1]
    density = centre[0]
    strain = [
        [
            0.5 * (slopes[left_index][1 + right_index] + slopes[right_index][1 + left_index])
            for right_index in range(3)
        ]
        for left_index in range(3)
    ]
    divergence = strain[0][0] + strain[1][1] + strain[2][2]
    rate_sum = jnp.zeros_like(density)
    for left_index in range(3):
        for right_index in range(3):
            entry = strain[left_index][right_index]
            if left_index == right_index:
                entry = entry - divergence / 3.0
            rate_sum = rate_sum + entry * entry
    shear_rate = jnp.sqrt(2.0 * rate_sum + 0.01)
    pressure = (stress[0] + stress[3] + stress[5]) / 3.0
    deviator = (
        (stress[0] - pressure) ** 2
        + (stress[3] - pressure) ** 2
        + (stress[5] - pressure) ** 2
        + 2.0 * (stress[1] ** 2 + stress[2] ** 2 + stress[4] ** 2)
    )
    shear_stress = jnp.sqrt(0.5 * deviator + 0.01)
    pressure_scale = jnp.sqrt(pressure * pressure + 1.0)
    friction = shear_stress / pressure_scale
    inertial = shear_rate / jnp.sqrt(pressure_scale)
    features = [
        density,
        pressure / pressure_scale,
        shear_rate,
        inertial,
        divergence,
        slopes[0][0],
        slopes[1][0],
        slopes[2][0],
    ]
    library_terms = list(features)
    for left_index in range(8):
        for right_index in range(left_index, 8):
            library_terms.append(features[left_index] * features[right_index])
    for left_index in range(1, 5):
        library_terms.append(features[left_index] ** 3)
    return (friction, jnp.stack(library_terms))


def seal_depth(extended, dim_depth):
    depth_index = lax.axis_index("depth")
    depth_count = lax.axis_size("depth")
    places = lax.broadcasted_iota(jnp.int32, extended.shape, dim_depth)
    lowest = jnp.logical_and(places == 0, depth_index == 0)
    highest = jnp.logical_and(
        places == extended.shape[dim_depth] - 1, depth_index == depth_count - 1
    )
    return jnp.where(jnp.logical_or(lowest, highest), jnp.zeros_like(extended), extended)


def share_ghosts(state):
    grown = with_halo(state, (("down", 1), ("cross", 2), ("depth", 3)), 1)
    return seal_depth(grown, 3)


def body(positions, velocities, sphere_radii, counts, coefficients):
    slot_ids = lax.broadcasted_iota(jnp.int32, sphere_radii.shape, 3)
    live_slots = (slot_ids < counts[..., None]).astype(jnp.float32)
    sphere_mass = live_slots * (sphere_radii / RADIUS_REF) ** 3
    safe_mass = sphere_mass + 1.0 - live_slots
    state_start = jnp.concatenate(
        [positions, velocities, sphere_radii[None], live_slots[None]], axis=0
    )
    force_start, unused = contact(share_ghosts(state_start))
    velocity_new = velocities + TIME_STEP * force_start / safe_mass
    position_new = positions + TIME_STEP * velocity_new
    state_next = jnp.concatenate(
        [position_new, velocity_new, sphere_radii[None], live_slots[None]], axis=0
    )
    extended = share_ghosts(state_next)
    force_next, stress = contact(extended)
    moments = jnp.concatenate([sphere_mass[None], sphere_mass * velocity_new, stress], axis=0)
    moment_rim = seal_depth(with_halo(moments, (("down", 1), ("cross", 2), ("depth", 3)), 1), 3)
    fields = coarse(extended, moment_rim)
    density = fields[0]
    node_values = jnp.concatenate([density[None], fields[1:4] / (density + MASS_SHIFT)], axis=0)
    padded = seal_depth(with_halo(node_values, (("down", 1), ("cross", 2), ("depth", 3)), 1), 3)
    friction, library_terms = library(padded, fields[4:10])
    residual_field = friction - jnp.sum(coefficients[:, None, None, None] * library_terms, axis=0)
    node_total = (
        friction.size * lax.axis_size("down") * lax.axis_size("cross") * lax.axis_size("depth")
    )
    gram_local = (
        jnp.einsum("kxyz,lxyz->kl", library_terms, library_terms, precision=lax.Precision.HIGHEST)
        / node_total
    )
    moment_local = (
        jnp.einsum("kxyz,xyz->k", library_terms, friction, precision=lax.Precision.HIGHEST)
        / node_total
    )
    gram_matrix, moment_vector = lax.psum((gram_local, moment_local), ("down", "cross", "depth"))
    return (velocity_new, force_next, residual_field, gram_matrix, moment_vector)


def solution(mesh):
    return jax.shard_map(
        body,
        mesh=mesh,
        in_specs=(
            P(None, ("groups", "down"), "cross", "depth", None),
            P(None, ("groups", "down"), "cross", "depth", None),
            P(("groups", "down"), "cross", "depth", None),
            P(("groups", "down"), "cross", "depth"),
            P(),
        ),
        out_specs=(
            P(None, ("groups", "down"), "cross", "depth", None),
            P(None, ("groups", "down"), "cross", "depth", None),
            P(("groups", "down"), "cross", "depth"),
            P("groups", None),
            P("groups"),
        ),
        check_vma=False,
    )
```

profile of v0, /device:TPU:0, one launch (start us, length us, event | category | flops | bytes accessed | tf_op | source)
XLA Modules:
  0.0 442.6 jit_solution(4039070204299480492)
XLA Ops:
  3.6 3.1 collective-permute-start
  65.8 2.9 fusion.2
  68.8 2.7 fusion.824
  71.6 6.3 %fusion.32 = (f32[2,2,2,128,128]{4,3,2,1,0:T(8,128)S(1)}, f32[2,2,2,128,128]{4,3,2,1,0:T(8,128)S(1)}, f32[2,2,2,128,128]{4,3,2,1,0:T(8,128)}, f32[2,2,2,128,128]...) fusion(f32[3,2,2,2,128]{4,3,2,1,0:T(2,128)S(1)} %copy.520, ...), kind=kLoop, calls=%fused_computation.140 | loop fusion | flops 16777216 | bytes 8609792 | tf_op jit(solution)/shard_map/reduce_sum | solution.py:56
  82.6 3.1 convolution_bitcast_fusion.17
  85.7 2.7 stack.242
  91.1 2.7 stack.248
  93.8 2.7 stack.244
  101.9 2.7 stack.260
  107.2 2.7 stack.256
  112.6 2.7 stack.252
  122.3 4.8 %fusion.18 = (f32[2,2,2,128,128]{4,3,2,1,0:T(8,128)S(1)}, f32[2,2,2,128,128]{4,3,2,1,0:T(8,128)S(1)}, f32[2,2,2,128,128]{4,3,2,1,0:T(8,128)S(1)}, f32[2,2,2,128,...) fusion(f32[3,2,2,2,128]{4,3,2,1,0:T(2,128)S(1)} %copy-done.71, ...), kind=kLoop, calls=%fused_computation.126 | loop fusion | flops 16777216 | bytes 8609792 | tf_op jit(solution)/shard_map/reduce_sum | solution.py:56
  149.9 8.1 %fusion.34 = (f32[2,2,2,128,128]{4,3,2,1,0:T(8,128)}, f32[2,2,2,128,128]{4,3,2,1,0:T(8,128)}, f32[2,2,2,128,128]{4,3,2,1,0:T(8,128)}, f32[2,2,2,128,128]{4,3,2,1...) fusion(f32[3,2,2,2,128]{4,3,2,1,0:T(2,128)S(1)} %copy-done.39, ...), kind=kLoop, calls=%fused_computation.142 | loop fusion | flops 18874368 | bytes 9658368 | tf_op jit(solution)/shard_map/reduce_sum | solution.py:56
  161.0 3.1 convolution_bitcast_fusion.16
  165.0 3.1 convolution_bitcast_fusion.15
  169.0 3.1 convolution_bitcast_fusion.14
  173.0 3.1 convolution_bitcast_fusion.13
  176.4 3.1 convolution_bitcast_fusion.12
  179.7 3.1 convolution_bitcast_fusion.11
  183.7 3.1 convolution_bitcast_fusion.10
  272.1 4.4 fusion.72
  287.3 5.7 %fusion.86 = (f32[2,2,2,128,128]{4,3,2,1,0:T(8,128)S(1)}, f32[2,2,2,128,128]{4,3,2,1,0:T(8,128)S(1)}, f32[2,2,2,128,128]{4,3,2,1,0:T(8,128)}, f32[2,2,2,128,128]...) fusion(f32[3,2,2,2,128]{4,3,2,1,0:T(2,128)S(1)} %copy-done.62, ...), kind=kLoop, calls=%fused_computation.194 | loop fusion | flops 16777216 | bytes 8609792 | tf_op jit(solution)/shard_map/reduce_sum | solution.py:56
  297.0 8.1 %fusion.88 = (f32[2,2,2,128,128]{4,3,2,1,0:T(8,128)}, f32[2,2,2,128,128]{4,3,2,1,0:T(8,128)}, f32[2,2,2,128,128]{4,3,2,1,0:T(8,128)}, f32[2,2,2,128,128]{4,3,2,1...) fusion(f32[3,2,2,2,128]{4,3,2,1,0:T(2,128)S(1)} %copy-done.50, ...), kind=kLoop, calls=%fused_computation.196 | loop fusion | flops 18874368 | bytes 9658368 | tf_op jit(solution)/shard_map/reduce_sum | solution.py:56
  315.6 3.1 convolution_bitcast_fusion.5
  318.9 3.1 convolution_bitcast_fusion.4
  322.3 3.1 convolution_bitcast_fusion.3
  325.7 3.1 convolution_bitcast_fusion.2
  329.0 3.1 convolution_bitcast_fusion.1
  332.6 3.1 convolution_bitcast_fusion
  344.4 2.7 collective-permute-start.13
  351.1 2.7 collective-permute-done.14
  380.1 62.1 %all-reduce = (f32[48,48]{1,0:T(8,128)}, f32[48]{0:T(128)}) all-reduce(f32[48,48]{1,0:T(8,128)S(1)} %fusion.130, f32[48]{0:T(128)S(1)} %fusion.131), channel_id=1, replica_groups=mesh['groups'=2,'down'=4,'cross'=2,'depth'=2] {'down','cross','depth'}, use_global_device_ids=true, to_apply=%region_136.137 | all-reduce | flops 2352 | bytes 18816 | tf_op jit(solution)/shard_map/psum | solution.py:229
  (1565 shorter events, 260.7 us)
Async XLA Ops:
  3.6 6.9 %collective-permute-start = (f32[8,1,2,2,128]{4,0,3,2,1:T(8,128)S(1)}, f32[8,1,2,2,128]{4,0,3,2,1:T(8,128)S(1)}, u32[]{:S(2)}, u32[]{:S(2)}) collective-permute-start(f32[8,1,2,2,128]{4,0,3,2,1:T(8,128)S(1)} %get-tuple-element.879), channel_id=1, source_target_pairs={{0,4},{4,8},{8,12},{12,0},{1,5},{5,9},{9,13},{13,1},{2,6},{6,10},{... | collective-permute-start | bytes 49160 | tf_op jit(solution)/shard_map/ppermute | solution.py:32
  6.6 3.9 collective-permute-start.1
  11.3 4.0 collective-permute-start.2
  12.9 3.9 collective-permute-start.3
  16.8 1.3 collective-permute-start.4
  16.9 1.4 collective-permute-start.5
  32.0 16.6 %copy-start.180 = (f32[1,2,2,2,128]{4,0,3,2,1:T(1,128)}, f32[1,2,2,2,128]{4,0,3,2,1:T(1,128)S(1)}, u32[]{:S(2)}) copy-start(f32[1,2,2,2,128]{4,0,3,2,1:T(1,128)S(1)} %get-tuple-element.744) | copy-start | bytes 12292
  32.0 16.6 %copy-start.182 = (f32[1,2,2,2,128]{4,0,3,2,1:T(1,128)}, f32[1,2,2,2,128]{4,0,3,2,1:T(1,128)S(1)}, u32[]{:S(2)}) copy-start(f32[1,2,2,2,128]{4,0,3,2,1:T(1,128)S(1)} %get-tuple-element.745) | copy-start | bytes 12292
  85.7 18.9 %copy-start.161 = (f32[1,2,2,2,128]{4,0,3,2,1:T(1,128)S(1)}, f32[1,2,2,2,128]{4,0,3,2,1:T(1,128)}, u32[]{:S(2)}) copy-start(f32[1,2,2,2,128]{4,0,3,2,1:T(1,128)} %copy-done.160) | copy-start | bytes 12292
  85.7 18.9 %copy-start.163 = (f32[1,2,2,2,128]{4,0,3,2,1:T(1,128)S(1)}, f32[1,2,2,2,128]{4,0,3,2,1:T(1,128)}, u32[]{:S(2)}) copy-start(f32[1,2,2,2,128]{4,0,3,2,1:T(1,128)} %copy-done.162) | copy-start | bytes 12292
  85.7 18.8 %copy-start.165 = (f32[1,2,2,2,128]{4,0,3,2,1:T(1,128)S(1)}, f32[1,2,2,2,128]{4,0,3,2,1:T(1,128)}, u32[]{:S(2)}) copy-start(f32[1,2,2,2,128]{4,0,3,2,1:T(1,128)} %copy-done.164) | copy-start | bytes 12292
  91.1 24.2 %copy-start.181 = (f32[1,2,2,2,128]{4,0,3,2,1:T(1,128)S(1)}, f32[1,2,2,2,128]{4,0,3,2,1:T(1,128)}, u32[]{:S(2)}) copy-start(f32[1,2,2,2,128]{4,0,3,2,1:T(1,128)} %copy-done.180) | copy-start | bytes 12292
  91.1 24.2 %copy-start.183 = (f32[1,2,2,2,128]{4,0,3,2,1:T(1,128)S(1)}, f32[1,2,2,2,128]{4,0,3,2,1:T(1,128)}, u32[]{:S(2)}) copy-start(f32[1,2,2,2,128]{4,0,3,2,1:T(1,128)} %copy-done.182) | copy-start | bytes 12292
  91.1 24.2 %copy-start.185 = (f32[1,2,2,2,128]{4,0,3,2,1:T(1,128)S(1)}, f32[1,2,2,2,128]{4,0,3,2,1:T(1,128)}, u32[]{:S(2)}) copy-start(f32[1,2,2,2,128]{4,0,3,2,1:T(1,128)} %copy-done.184) | copy-start | bytes 12292
  205.4 5.7 %collective-permute-start.6 = (f32[8,1,2,2,128]{4,0,3,2,1:T(8,128)S(1)}, f32[8,1,2,2,128]{4,0,3,2,1:T(8,128)S(1)}, u32[]{:S(2)}, u32[]{:S(2)}) collective-permute-start(f32[8,1,2,2,128]{4,0,3,2,1:T(8,128)S(1)} %get-tuple-element.877), channel_id=1, source_target_pairs={{0,4},{4,8},{8,12},{12,0},{1,5},{5,9},{9,13},{13,1},{2,6},{6,10},{... | collective-permute-start | bytes 49160 | tf_op jit(solution)/shard_map/ppermute | solution.py:32
  206.8 4.3 collective-permute-start.7
  211.2 4.0 collective-permute-start.8
  211.6 3.9 collective-permute-start.9
  215.6 1.3 collective-permute-start.10
  215.6 1.4 collective-permute-start.11
  343.1 5.8 %collective-permute-start.12 = (f32[10,1,2,2,128]{4,0,3,2,1:T(8,128)S(1)}, f32[10,1,2,2,128]{4,0,3,2,1:T(8,128)S(1)}, u32[]{:S(2)}, u32[]{:S(2)}) collective-permute-start(f32[10,1,2,2,128]{4,0,3,2,1:T(8,128)S(1)} %get-tuple-element.857), channel_id=1, source_target_pairs={{0,4},{4,8},{8,12},{12,0},{1,5},{5,9},{9,13},{13,1},{2,6},{6,10},{... | collective-permute-start | bytes 61448 | tf_op jit(solution)/shard_map/ppermute | solution.py:32
  344.4 4.6 %collective-permute-start.13 = (f32[10,1,2,2,128]{4,0,3,2,1:T(8,128)S(1)}, f32[10,1,2,2,128]{4,0,3,2,1:T(8,128)S(1)}, u32[]{:S(2)}, u32[]{:S(2)}) collective-permute-start(f32[10,1,2,2,128]{4,0,3,2,1:T(8,128)S(1)} %get-tuple-element.858), channel_id=1, source_target_pairs={{4,0},{8,4},{12,8},{0,12},{5,1},{9,5},{13,9},{1,13},{6,2},{10,6},{... | collective-permute-start | bytes 61448 | tf_op jit(solution)/shard_map/ppermute | solution.py:33
  349.0 4.8 %collective-permute-start.14 = (f32[10,4,1,2,128]{4,0,3,2,1:T(8,128)S(1)}, f32[10,4,1,2,128]{4,0,3,2,1:T(8,128)S(1)}, u32[]{:S(2)}, u32[]{:S(2)}) collective-permute-start(f32[10,4,1,2,128]{4,0,3,2,1:T(8,128)S(1)} %get-tuple-element.851), channel_id=1, source_target_pairs={{0,2},{2,0},{1,3},{3,1},{4,6},{6,4},{5,7},{7,5},{8,10},{10,8},{9,1... | collective-permute-start | bytes 122888 | tf_op jit(solution)/shard_map/ppermute | solution.py:32
  350.7 4.3 collective-permute-start.15
  355.0 1.4 collective-permute-start.16
  355.1 1.5 collective-permute-start.17
  361.3 5.5 %collective-permute-start.18 = (f32[4,1,2,2]{3,2,1,0:T(2,128)S(1)}, f32[4,1,2,2]{3,2,1,0:T(2,128)S(1)}, u32[]{:S(2)}, u32[]{:S(2)}) collective-permute-start(f32[4,1,2,2]{3,2,1,0:T(2,128)S(1)} %get-tuple-element.906), channel_id=1, source_target_pairs={{0,4},{4,8},{8,12},{12,0},{1,5},{5,9},{9,13},{13,1},{2,6},{6,10},{... | collective-permute-start | bytes 200 | tf_op jit(solution)/shard_map/ppermute | solution.py:32
  362.6 4.2 collective-permute-start.19
  366.8 3.7 collective-permute-start.20
  367.6 3.7 collective-permute-start.21
  371.3 1.2 collective-permute-start.22
  371.4 1.4 collective-permute-start.23
  (538 other events, 2121.0 us)
where the time goes:
time: 450 us; the launch traced here: 443 us
  local copies, waits for them, and re-layouts  126 us (28%)
  matrix products  115 us (26%)
  other arithmetic  83 us (18%)
  blocking collectives  62.1 us (14%)
  starting transfers between devices  27.6 us (6%)
  waiting for transfers between devices  19.3 us (4%)
  between operations  9.17 us (2%)
    dot_general x54, matrix products, contact(): jnp.einsum('xyzij,kxyzj->kxyzi', weight, columns, precision=lax.Precision...  115 us
    psum x1, blocking collectives, body(): lax.psum((gram_local, moment_local), ('down', 'cross', 'depth'))  62.1 us
    another operation x54, local copies, waits for them, and re-layouts, contact(): jnp.stack([jnp.ones_like(places[0]), places[0], places[1], places[2], pla...  59.6 us
    reduce_sum x8, other arithmetic, contact(): squared = jnp.sum(branch * branch, axis=0)  41.9 us
    slice x59, local copies, waits for them, and re-layouts, contact(): relative = centre[3:6, ..., :, None] - beside[3:6, ..., None, :]  28.6 us
    another operation x52, local copies, waits for them, and re-layouts, contact(): jnp.stack([beside[0] + shift_x, beside[1] + shift_y, beside[2] + shift_z])  23.7 us
    ppermute x12, starting transfers between devices, with_halo(): after = lax.ppermute(first, axis, down)  15.9 us
    ppermute x12, waiting for transfers between devices, with_halo(): before = lax.ppermute(last, axis, up)  14.8 us
  transfers between devices with their start and end apart: 24, of which 21 were waited for; matrix products, arithmetic and copies ran while one was open for 1% of the time, Pallas kernels for 0%

commit v1 on v0

v1 whole, which is shorter than its diff:
```python
import functools

import jax
import jax.numpy as jnp
from jax import lax
from jax.experimental import pallas as pl
from jax.experimental.pallas import tpu as pltpu
from jax.sharding import PartitionSpec as P

STIFFNESS = 100.0
DAMPING = 20.0
TIME_STEP = 0.05
KERNEL_WIDTH = 0.4
KERNEL_NORM = 64.0
SOFTENING = 0.0001
RADIUS_REF = 0.1
MASS_SHIFT = 0.1
DEAD = -1000.0
TERMS = 48
S = 128
F32 = jnp.float32
BF16 = jnp.bfloat16
PAIR_LIST = ((0, 0), (0, 1), (0, 2), (1, 1), (1, 2), (2, 2))
VMEM_SPEC = pl.BlockSpec(memory_space=pltpu.VMEM)
SMEM_SPEC = pl.BlockSpec(memory_space=pltpu.SMEM)
VMEM_LIMIT = 48 * 1024 * 1024


def split3(value):
    high = value.astype(BF16).astype(F32)
    rest = value - high
    middle = rest.astype(BF16).astype(F32)
    return high, middle, rest - middle


def row_ids(shape):
    return lax.broadcasted_iota(jnp.int32, shape, 0)


def pack_kernel(counts, positions, velocities, radii, own, inner):
    depth = lax.axis_index("depth")
    lanes = lax.broadcasted_iota(jnp.int32, (1, S), 1)
    for a in range(2):
        for b in range(2):
            for z in range(2):
                for k in range(3):
                    own[a, b, z, k : k + 1, :] = positions[k, a, b, z : z + 1, :]
                    own[a, b, z, 3 + k : 4 + k, :] = velocities[k, a, b, z : z + 1, :]
                live = lanes < counts[a, b, z]
                own[a, b, z, 6:7, :] = jnp.where(live, radii[a, b, z : z + 1, :], DEAD)
                own[a, b, z, 7:8, :] = jnp.zeros((1, S), F32)
            inner[a, b] = own[a, b, 1 - depth]


def local_state(raw, centre):
    rows = row_ids(raw.shape)
    shift = jnp.where(rows == 0, centre[0], jnp.where(rows == 1, centre[1], centre[2]))
    return jnp.where(rows < 3, raw + shift, raw)


def dots_of(state):
    p = [state[k : k + 1] for k in range(3)]
    v = [state[3 + k : 4 + k] for k in range(3)]
    square = p[0] * p[0] + p[1] * p[1] + p[2] * p[2]
    cross = p[0] * v[0] + p[1] * v[1] + p[2] * v[2]
    return square, cross


def neighbour_side(raw, centre, with_stress):
    state = local_state(raw, centre)
    rows = row_ids(state.shape)
    square, cross = dots_of(state)
    features = jnp.where(rows == 6, square, jnp.where(rows == 7, cross, state))
    high, middle, low = split3(features)
    ones = jnp.where(rows < 3, 1.0, 0.0).astype(F32)
    radius = jnp.where(rows == 0, raw[6:7], 0.0)
    stacked = jnp.concatenate([high, high, high, middle, middle, low, ones, radius], axis=0)
    turned = jnp.transpose(stacked)
    spread = jnp.broadcast_to(turned[:, 56:57], (S, S))
    p = [state[k : k + 1] for k in range(3)]
    first = jnp.where(
        rows == 0, 1.0, jnp.where(rows == 1, p[0], jnp.where(rows == 2, p[1], jnp.where(rows == 3, p[2], 0.0)))
    )
    if with_stress:
        for place, (left, right) in enumerate(PAIR_LIST[:4]):
            first = jnp.where(rows == 4 + place, p[left] * p[right], first)
        second = jnp.where(rows == 0, p[1] * p[2], jnp.where(rows == 1, p[2] * p[2], 0.0))
        first = jnp.concatenate([first, second], axis=0)
    parts = list(split3(first))
    if not with_stress:
        parts.append(jnp.zeros_like(first))
    columns = jnp.concatenate(parts, axis=0).astype(BF16)
    return turned.astype(BF16), spread, jnp.concatenate([columns, columns], axis=1)


def centre_side(state):
    rows = row_ids(state.shape)
    square, cross = dots_of(state)
    turned = pltpu.roll(state, 3, 0)
    back = pltpu.roll(state, 5, 0)
    near = jnp.where(rows < 3, -2.0 * state, jnp.where(rows == 6, 1.0, 0.0))
    pull = jnp.where(
        rows < 3,
        DAMPING * back,
        jnp.where(rows < 6, DAMPING * turned, jnp.where(rows == 7, -DAMPING, 0.0)),
    )
    out = []
    for table, constant in ((near, square + SOFTENING), (pull, -DAMPING * cross)):
        high, middle, low = split3(table)
        c_high, c_middle, c_low = split3(constant)
        tail = jnp.where(
            rows == 0, c_high, jnp.where(rows == 1, c_middle, jnp.where(rows == 2, c_low, 0.0))
        )
        out.append(
            jnp.concatenate(
                [high, middle, low, high, middle, high, tail, jnp.zeros_like(tail)], axis=0
            ).astype(BF16)
        )
    return out


def pair_tile(left, spread, columns, right, radius, self_lane):
    width = radius.shape[1]
    product = lax.dot_general(
        left, right, (((1,), (0,)), ((), ())), preferred_element_type=F32
    )
    squared = jnp.maximum(product[:, :width], SOFTENING)
    inverse = lax.rsqrt(squared)
    reach = jnp.concatenate([spread] * (width // S), axis=1) + radius
    weight = jnp.maximum(reach * inverse - 1.0, 0.0) * (
        STIFFNESS + product[:, width:] * inverse
    )
    if self_lane is not None:
        lanes = lax.broadcasted_iota(jnp.int32, weight.shape, 1)
        weight = jnp.where(lanes == row_ids(weight.shape) + self_lane, 0.0, weight)
    high = weight.astype(BF16)
    low = (weight - high.astype(F32)).astype(BF16)
    return lax.dot_general(
        columns,
        jnp.concatenate([high, low], axis=0),
        (((1,), (0,)), ((), ())),
        preferred_element_type=F32,
    )


def neighbour_cells(pieces):
    own, depth_halo, cross_before, cross_after, diag_before, diag_after, x_before, x_after = pieces

    def cell(x, y, slot):
        if x in (0, 3):
            face = x_before if x == 0 else x_after
            if y in (1, 2):
                return face[(y - 1) * 2 + slot] if slot < 2 else face[4 + y - 1]
            side = 6 if y == 0 else 8
            return face[side + slot] if slot < 2 else face[10 + (0 if y == 0 else 1)]
        if y in (1, 2):
            return own[x - 1, y - 1, slot] if slot < 2 else depth_halo[x - 1, y - 1]
        if slot < 2:
            return (cross_before if y == 0 else cross_after)(x - 1, slot)
        return (diag_before if y == 0 else diag_after)(x - 1)

    return cell


def contact_all(cell, depth, with_stress, left_ref, spread_ref, columns_ref, finish, radius_of):
    halo_z = 1.5 - 3.0 * depth.astype(F32)
    for x in range(4):
        for y in range(4):
            for slot in range(3):
                centre = (x - 1.5, y - 1.5, slot - 0.5 if slot < 2 else halo_z)
                place = (x * 4 + y) * 3 + slot
                left, spread, columns = neighbour_side(cell(x, y, slot), centre, with_stress)
                left_ref[place] = left
                spread_ref[place] = spread
                columns_ref[place] = columns
    inner = 1 - depth

    def one_column(step, carry):
        a = step // 2
        b = step % 2
        raws = [radius_of[a, b, z] for z in range(2)]
        states = []
        for z in range(2):
            states.append(
                local_state(raws[z], (a.astype(F32) - 0.5, b.astype(F32) - 0.5, z - 0.5))
            )
        sides = [centre_side(state) for state in states]
        right = jnp.concatenate([sides[0][0], sides[1][0], sides[0][1], sides[1][1]], axis=1)
        radius = jnp.concatenate([raws[0][6:7], raws[1][6:7]], axis=1)
        total = None
        for dx in range(3):
            for dy in range(3):
                for slot in range(2):
                    place = ((a + dx) * 4 + (b + dy)) * 3 + slot
                    self_lane = slot * S if (dx == 1 and dy == 1) else None
                    part = pair_tile(
                        left_ref[place], spread_ref[place], columns_ref[place], right, radius, self_lane
                    )
                    total = part if total is None else total + part
        upper = inner == 1
        right_inner = jnp.concatenate(
            [jnp.where(upper, sides[1][k].astype(F32), sides[0][k].astype(F32)).astype(BF16) for k in range(2)],
            axis=1,
        )
        radius_inner = jnp.where(upper, raws[1][6:7], raws[0][6:7])
        extra = None
        for dx in range(3):
            for dy in range(3):
                place = ((a + dx) * 4 + (b + dy)) * 3 + 2
                part = pair_tile(
                    left_ref[place],
                    spread_ref[place],
                    columns_ref[place],
                    right_inner,
                    radius_inner,
                    None,
                )
                extra = part if extra is None else extra + part
        rows = 16 if with_stress else 8
        total = total[:rows] + total[rows : 2 * rows] + total[2 * rows : 3 * rows]
        extra = extra[:rows] + extra[rows : 2 * rows] + extra[2 * rows : 3 * rows]
        for z in range(2):
            sums = total[:, z * S : (z + 1) * S] + jnp.where(inner == z, extra, 0.0)
            finish(a, b, z, raws[z], states[z], sums)
        return carry

    lax.fori_loop(0, 4, one_column, 0)


def force_of(state, sums):
    return [state[k : k + 1] * sums[0:1] - sums[1 + k : 2 + k] for k in range(3)]


def unpack_pieces(refs, wide):
    own, depth_halo = refs[0], refs[1]
    if wide:
        cb, ca, db, da, xb, xa = refs[2:8]
        return (
            own,
            depth_halo,
            lambda x, slot: cb[x, slot],
            lambda x, slot: ca[x, slot],
            lambda x: db[x],
            lambda x: da[x],
            xb,
            xa,
        )
    cross, diag, xb, xa = refs[2:6]
    return (
        own,
        depth_halo,
        lambda x, slot: cross[x, 1, slot],
        lambda x, slot: cross[x, 0, slot],
        lambda x: diag[x, 1],
        lambda x: diag[x, 0],
        xb,
        xa,
    )


def step_kernel(wide, *refs):
    count = 8 if wide else 6
    pieces = unpack_pieces(refs[:count], wide)
    velocity_out, own_out, inner_out, left_ref, spread_ref, columns_ref = refs[count:]
    depth = lax.axis_index("depth")
    own = pieces[0]

    def finish(a, b, z, raw, state, sums):
        force = force_of(state, sums)
        radius = raw[6:7]
        live = radius > 0.0
        scaled = radius / RADIUS_REF
        safe_mass = jnp.where(live, scaled * scaled * scaled, 1.0)
        for k in range(3):
            velocity = raw[3 + k : 4 + k] + TIME_STEP * force[k] / safe_mass
            position = raw[k : k + 1] + TIME_STEP * velocity
            velocity_out[k, a, b, z : z + 1, :] = velocity
            own_out[a, b, z, k : k + 1, :] = position
            own_out[a, b, z, 3 + k : 4 + k, :] = velocity
        own_out[a, b, z, 6:8, :] = raw[6:8]

    contact_all(
        neighbour_cells(pieces), depth, False, left_ref, spread_ref, columns_ref, finish, own
    )
    for a in range(2):
        for b in range(2):
            inner_out[a, b] = own_out[a, b, 1 - depth]


def field_kernel(wide, grid, *refs):
    count = 8 if wide else 6
    pieces = unpack_pieces(refs[:count], wide)
    force_out, node_out, left_ref, spread_ref, columns_ref = refs[count:]
    depth = lax.axis_index("depth")
    down = lax.axis_index("down")
    cross = lax.axis_index("cross")
    own = pieces[0]
    size_x, size_y, size_z = grid
    nodes = size_x * size_y * size_z
    node_out[...] = jnp.zeros((16, nodes), F32)
    rows32 = lax.broadcasted_iota(jnp.int32, (32, 1), 0)
    shift = [rows32 // 9 - 1, (rows32 // 3) % 3 - 1, rows32 % 3 - 1]
    lanes = lax.broadcasted_iota(jnp.int32, (1, nodes), 1)
    node_x = lanes // (size_y * size_z)
    node_y = (lanes // size_z) % size_y
    node_z = lanes % size_z

    def finish(a, b, z, raw, state, sums):
        force = force_of(state, sums)
        for k in range(3):
            force_out[k, a, b, z : z + 1, :] = force[k]
        x = [state[k : k + 1] for k in range(3)]
        radius = raw[6:7]
        scaled = radius / RADIUS_REF
        mass = jnp.where(radius > 0.0, scaled * scaled * scaled, 0.0)
        rows = [mass] + [mass * raw[3 + k : 4 + k] for k in range(3)]
        for pair_id, (left, right) in enumerate(PAIR_LIST):
            rows.append(
                0.5
                * (
                    x[left] * x[right] * sums[0:1]
                    - x[left] * sums[1 + right : 2 + right]
                    - x[right] * sums[1 + left : 2 + left]
                    + sums[4 + pair_id : 5 + pair_id]
                )
            )
        moments = jnp.concatenate(rows + [jnp.zeros((6, S), F32)], axis=0)
        place = [raw[k : k + 1] + shift[k].astype(F32) for k in range(3)]
        squared = place[0] * place[0] + place[1] * place[1] + place[2] * place[2]
        kernel = jnp.exp(squared * (-0.5 / (KERNEL_WIDTH * KERNEL_WIDTH))) / KERNEL_NORM
        kernel = jnp.where(rows32 < 27, kernel, 0.0)
        parts = lax.dot_general(
            moments,
            kernel,
            (((1,), (1,)), ((), ())),
            precision=lax.Precision.HIGHEST,
            preferred_element_type=F32,
        )
        target_x = (down * 2 + a - shift[0] + size_x) % size_x
        target_y = (cross * 2 + b - shift[1] + size_y) % size_y
        target_z = depth * 2 + z - shift[2]
        chosen = jnp.logical_and(
            jnp.logical_and(node_x == target_x, node_y == target_y), node_z == target_z
        )
        chosen = jnp.where(chosen, 1.0, 0.0).astype(F32)
        node_out[...] += lax.dot_general(
            parts,
            chosen,
            (((1,), (0,)), ((), ())),
            precision=lax.Precision.HIGHEST,
            preferred_element_type=F32,
        )

    contact_all(
        neighbour_cells(pieces), depth, True, left_ref, spread_ref, columns_ref, finish, own
    )


def library_kernel(grid, count, coefficients, *refs):
    parts = [ref[...] for ref in refs[:count]]
    residual_out, gram_out, moment_out, terms = refs[count:]
    while len(parts) > 1:
        parts = [parts[k] + parts[k + 1] for k in range(0, len(parts), 2)]
    fields = parts[0]
    size_x, size_y, size_z = grid
    nodes = size_x * size_y * size_z
    lanes = lax.broadcasted_iota(jnp.int32, (1, nodes), 1)
    node_x = lanes // (size_y * size_z)
    node_y = (lanes // size_z) % size_y
    node_z = lanes % size_z
    rows = row_ids((8, nodes))
    density = fields[0:1]
    values = jnp.where(rows == 0, fields[0:8], fields[0:8] / (density + MASS_SHIFT))

    def moved(value, step):
        return pltpu.roll(value, step % nodes, 1)

    plane = size_y * size_z
    slope_x = (moved(values, -plane) - moved(values, plane)) * 0.5
    after_y = jnp.where(
        node_y == size_y - 1, moved(values, (size_y - 1) * size_z), moved(values, -size_z)
    )
    before_y = jnp.where(
        node_y == 0, moved(values, -(size_y - 1) * size_z), moved(values, size_z)
    )
    slope_y = (after_y - before_y) * 0.5
    after_z = jnp.where(node_z == size_z - 1, 0.0, moved(values, -1))
    before_z = jnp.where(node_z == 0, 0.0, moved(values, 1))
    slope_z = (after_z - before_z) * 0.5
    slopes = [[table[k : k + 1] for k in range(4)] for table in (slope_x, slope_y, slope_z)]
    strain = [
        [0.5 * (slopes[left][1 + right] + slopes[right][1 + left]) for right in range(3)]
        for left in range(3)
    ]
    divergence = strain[0][0] + strain[1][1] + strain[2][2]
    rate_sum = jnp.zeros_like(density)
    for left in range(3):
        for right in range(3):
            entry = strain[left][right]
            if left == right:
                entry = entry - divergence / 3.0
            rate_sum = rate_sum + entry * entry
    shear_rate = jnp.sqrt(2.0 * rate_sum + 0.01)
    stress = [fields[4 + k : 5 + k] for k in range(6)]
    pressure = (stress[0] + stress[3] + stress[5]) / 3.0
    deviator = (
        (stress[0] - pressure) ** 2
        + (stress[3] - pressure) ** 2
        + (stress[5] - pressure) ** 2
        + 2.0 * (stress[1] ** 2 + stress[2] ** 2 + stress[4] ** 2)
    )
    shear_stress = jnp.sqrt(0.5 * deviator + 0.01)
    pressure_scale = jnp.sqrt(pressure * pressure + 1.0)
    friction = shear_stress / pressure_scale
    features = [
        density,
        pressure / pressure_scale,
        shear_rate,
        shear_rate / jnp.sqrt(pressure_scale),
        divergence,
        slopes[0][0],
        slopes[1][0],
        slopes[2][0],
    ]
    entries = list(features)
    for left in range(8):
        for right in range(left, 8):
            entries.append(features[left] * features[right])
    for left in range(1, 5):
        entries.append(features[left] * features[left] * features[left])
    model = jnp.zeros_like(density)
    for k, entry in enumerate(entries):
        terms[k : k + 1, :] = entry
        model = model + coefficients[k] * entry
    residual = friction - model
    table = terms[...]
    gram_out[...] = (
        lax.dot_general(
            table,
            table,
            (((1,), (1,)), ((), ())),
            precision=lax.Precision.HIGHEST,
            preferred_element_type=F32,
        )
        / nodes
    )
    moment = lax.dot_general(
        jnp.broadcast_to(friction, (8, nodes)),
        table,
        (((1,), (1,)), ((), ())),
        precision=lax.Precision.HIGHEST,
        preferred_element_type=F32,
    )
    moment_out[...] = moment[0:1] / nodes
    down = lax.axis_index("down")
    cross = lax.axis_index("cross")
    depth = lax.axis_index("depth")
    b_rows = lax.broadcasted_iota(jnp.int32, (2, 1), 0)
    z_lanes = lax.broadcasted_iota(jnp.int32, (2, 2), 1)
    for a in range(2):
        mine = jnp.logical_and(node_x == down * 2 + a, node_y == cross * 2 + b_rows)
        column = [
            jnp.sum(
                jnp.where(jnp.logical_and(mine, node_z == depth * 2 + z), residual, 0.0),
                axis=1,
                keepdims=True,
            )
            for z in range(2)
        ]
        residual_out[a] = jnp.where(z_lanes == 0, column[0], column[1])


def ring(axis, step):
    peers = lax.axis_size(axis)
    return [(i, (i + step) % peers) for i in range(peers)]


def exchange(own, inner):
    cross = lax.axis_size("cross")
    depth_halo = lax.ppermute(inner, "depth", [(0, 1), (1, 0)])
    if cross == 2:
        side = lax.ppermute(own, "cross", [(0, 1), (1, 0)])
        diag = lax.ppermute(inner, ("cross", "depth"), [(i, 3 - i) for i in range(4)])
        sides = [side, diag]

        def face(x):
            return jnp.concatenate(
                [
                    own[x].reshape(4, 8, S),
                    depth_halo[x],
                    side[x, 1],
                    side[x, 0],
                    diag[x, 1][None],
                    diag[x, 0][None],
                ],
                axis=0,
            )

    else:
        pairs = [(i * 2 + j, ((i + 1) % cross) * 2 + 1 - j) for i in range(cross) for j in range(2)]
        back = [(i * 2 + j, ((i - 1) % cross) * 2 + 1 - j) for i in range(cross) for j in range(2)]
        before = lax.ppermute(own[:, 1], "cross", ring("cross", 1))
        after = lax.ppermute(own[:, 0], "cross", ring("cross", -1))
        diag_before = lax.ppermute(inner[:, 1], ("cross", "depth"), pairs)
        diag_after = lax.ppermute(inner[:, 0], ("cross", "depth"), back)
        sides = [before, after, diag_before, diag_after]

        def face(x):
            return jnp.concatenate(
                [
                    own[x].reshape(4, 8, S),
                    depth_halo[x],
                    before[x],
                    after[x],
                    diag_before[x][None],
                    diag_after[x][None],
                ],
                axis=0,
            )

    x_before = lax.ppermute(face(1), "down", ring("down", 1))
    x_after = lax.ppermute(face(0), "down", ring("down", -1))
    return [own, depth_halo] + sides + [x_before, x_after]


def shared(value, axes, peers):
    return [value] + [
        lax.ppermute(value, axes, [(i, i ^ k) for i in range(peers)]) for k in range(1, peers)
    ]


def tree_sum(parts):
    while len(parts) > 1:
        parts = [parts[k] + parts[k + 1] for k in range(0, len(parts), 2)]
    return parts[0]


def body(positions, velocities, sphere_radii, counts, coefficients):
    down, cross, depth = (lax.axis_size(name) for name in ("down", "cross", "depth"))
    wide = cross != 2
    grid = (2 * down, 2 * cross, 2 * depth)
    nodes = grid[0] * grid[1] * grid[2]
    params = pltpu.CompilerParams(vmem_limit_bytes=VMEM_LIMIT)
    state_shape = jax.ShapeDtypeStruct((2, 2, 2, 8, S), F32)
    inner_shape = jax.ShapeDtypeStruct((2, 2, 8, S), F32)
    vector_shape = jax.ShapeDtypeStruct((3, 2, 2, 2, S), F32)
    own, inner = pl.pallas_call(
        pack_kernel,
        out_shape=(state_shape, inner_shape),
        in_specs=[SMEM_SPEC, VMEM_SPEC, VMEM_SPEC, VMEM_SPEC],
        out_specs=(VMEM_SPEC, VMEM_SPEC),
        compiler_params=params,
        name="pack",
    )(counts, positions, velocities, sphere_radii)

    def scratch(rows):
        return [
            pltpu.VMEM((48, S, 64), BF16),
            pltpu.VMEM((48, S, S), F32),
            pltpu.VMEM((48, rows, 2 * S), BF16),
        ]

    pieces = exchange(own, inner)
    velocity_new, own, inner = pl.pallas_call(
        functools.partial(step_kernel, wide),
        out_shape=(vector_shape, state_shape, inner_shape),
        in_specs=[VMEM_SPEC] * len(pieces),
        out_specs=(VMEM_SPEC,) * 3,
        scratch_shapes=scratch(32),
        compiler_params=params,
        name="step",
    )(*pieces)
    pieces = exchange(own, inner)
    force_next, partial = pl.pallas_call(
        functools.partial(field_kernel, wide, grid),
        out_shape=(vector_shape, jax.ShapeDtypeStruct((16, nodes), F32)),
        in_specs=[VMEM_SPEC] * len(pieces),
        out_specs=(VMEM_SPEC,) * 2,
        scratch_shapes=scratch(48),
        compiler_params=params,
        name="field",
    )(*pieces)
    partial = tree_sum(shared(partial, ("cross", "depth"), cross * depth))
    parts = shared(partial, "down", down)
    residual_field, gram_matrix, moment = pl.pallas_call(
        functools.partial(library_kernel, grid, len(parts)),
        out_shape=(
            jax.ShapeDtypeStruct((2, 2, 2), F32),
            jax.ShapeDtypeStruct((TERMS, TERMS), F32),
            jax.ShapeDtypeStruct((1, TERMS), F32),
        ),
        in_specs=[SMEM_SPEC] + [VMEM_SPEC] * len(parts),
        out_specs=(VMEM_SPEC,) * 3,
        scratch_shapes=[pltpu.VMEM((TERMS, nodes), F32)],
        compiler_params=params,
        name="library",
    )(coefficients, *parts)
    return (velocity_new, force_next, residual_field, gram_matrix, moment.reshape(TERMS))


def solution(mesh):
    return jax.shard_map(
        body,
        mesh=mesh,
        in_specs=(
            P(None, ("groups", "down"), "cross", "depth", None),
            P(None, ("groups", "down"), "cross", "depth", None),
            P(("groups", "down"), "cross", "depth", None),
            P(("groups", "down"), "cross", "depth"),
            P(),
        ),
        out_specs=(
            P(None, ("groups", "down"), "cross", "depth", None),
            P(None, ("groups", "down"), "cross", "depth", None),
            P(("groups", "down"), "cross", "depth"),
            P("groups", None),
            P("groups"),
        ),
        check_vma=False,
    )
```

time: 450 us -> 82.6 us (0.18); the launches traced: 443 us -> 82.3 us
  local copies, waits for them, and re-layouts: 126 us -> 2.82 us
  matrix products: 115 us -> 0 us
  other arithmetic: 83 us -> 0.01 us
  blocking collectives: 62.1 us -> 0 us
  Pallas kernels: 0 us -> 41.8 us
  starting transfers between devices: 27.6 us -> 17.3 us
  between operations: 9.17 us -> 0.73 us
    dot_general x56 -> x0, matrix products: 115 us -> none  [the longest x54 115 us: contact(): jnp.einsum('xyzij,kxyzj->kxyzi', weight, columns, precision=lax.Precision...]
    another operation x108 -> x0, local copies, waits for them, and re-layouts: 83.7 us -> none  [the longest x54 59.6 us: contact(): jnp.stack([jnp.ones_like(places[0]), places[0], places[1], places[2], pla...]
    psum x1 -> x0, blocking collectives: 62.1 us -> none  [body(): lax.psum((gram_local, moment_local), ('down', 'cross', 'depth'))]
    reduce_sum x12 -> x0, other arithmetic: 42.9 us -> none  [the longest x8 41.9 us: contact(): squared = jnp.sum(branch * branch, axis=0)]
    pallas_call x0 -> x4, Pallas kernels: none -> 41.8 us  [the longest x1 20.9 us: body(): pl.pallas_call(functools.partial(field_kernel, wide, grid), out_shape=(ve...]
    slice x80 -> x2, local copies, waits for them, and re-layouts: 29.2 us -> 0.01 us  [face(): own[x].reshape(4, 8, S)]
    mul x31 -> x0, other arithmetic: 13.7 us -> none  [the longest x6 3.38 us: contact(): places[1] * places[1]]
    ppermute x24 -> x16, starting transfers between devices: 27.6 us -> 17.3 us  [the longest x6 6.31 us: shared(): lax.ppermute(value, axes, [(i, i ^ k) for i in range(peers)])]
  transfers between devices with their start and end apart: 24 -> 16, of which waited for: 21 -> 11; matrix products, arithmetic and copies ran while one was open for 1% -> 0% of each run, Pallas kernels for 0% -> 0%
where the time goes in v1:
time: 82.6 us; the launch traced here: 82.3 us
  Pallas kernels  41.8 us (51%)
  waiting for transfers between devices  19.5 us (24%)
  starting transfers between devices  17.3 us (21%)
  local copies, waits for them, and re-layouts  2.82 us (3%)
    pallas_call x1, Pallas kernels, body(): pl.pallas_call(functools.partial(field_kernel, wide, grid), out_shape=(ve...  20.9 us
    pallas_call x1, Pallas kernels, body(): pl.pallas_call(functools.partial(step_kernel, wide), out_shape=(vector_sh...  18.8 us
    ppermute x6, starting transfers between devices, shared(): lax.ppermute(value, axes, [(i, i ^ k) for i in range(peers)])  6.31 us
    ppermute x2, waiting for transfers between devices, exchange(): x_before = lax.ppermute(face(1), 'down', ring('down', 1))  5.73 us
    ppermute x2, waiting for transfers between devices, exchange(): side = lax.ppermute(own, 'cross', [(0, 1), (1, 0)])  5.48 us
    ppermute x2, waiting for transfers between devices, exchange(): x_after = lax.ppermute(face(0), 'down', ring('down', -1))  4.09 us
    ppermute x2, starting transfers between devices, exchange(): x_after = lax.ppermute(face(0), 'down', ring('down', -1))  3.71 us
    ppermute x6, waiting for transfers between devices, shared(): lax.ppermute(value, axes, [(i, i ^ k) for i in range(peers)])  3.45 us
  transfers between devices with their start and end apart: 16, of which 11 were waited for; matrix products, arithmetic and copies ran while one was open for 0% of the time, Pallas kernels for 0%

profile of v1, /device:TPU:0, one launch (start us, length us, event | category | flops | bytes accessed | tf_op | source)
XLA Modules:
  0.0 82.3 jit_solution(13208047343182475114)
XLA Ops:
  0.6 0.7 copy-done
  1.3 0.7 copy-done.1
  2.0 0.7 copy-done.2
  2.7 0.7 copy-done.3
  3.4 0.6 pack.1
  4.0 2.4 %collective-permute-start.2 = (f32[2,2,8,128]{3,2,1,0:T(8,128)S(1)}, f32[2,2,8,128]{3,2,1,0:T(8,128)S(1)}, u32[]{:S(2)}, u32[]{:S(2)}) collective-permute-start(f32[2,2,8,128]{3,2,1,0:T(8,128)S(1)} %get-tuple-element.16), channel_id=1, source_target_pairs={{0,3},{1,2},{2,1},{3,0},{4,7},{5,6},{6,5},{7,4},{8,11},{9,10},{10,... | collective-permute-start | bytes 49160 | tf_op jit(solution)/shard_map/ppermute | solution.py:483
  6.5 0.7 collective-permute-start
  7.1 0.0 collective-permute-start.1
  7.2 0.8 collective-permute-done.refs_1_
  8.0 3.1 %collective-permute-done.1.refs_2_ = f32[2,2,2,8,128]{4,3,2,1,0:T(8,128)S(1)} collective-permute-done((f32[2,2,2,8,128]{4,3,2,1,0:T(8,128)S(1)}, f32[2,2,2,8,128]{4,3,2,1,0:T(8,128)S(1)}, u32[]{:S(2)}, u32[]{:S(2)}) %collective-permute-start.1) | collective-permute-done | bytes 32800 | tf_op jit(solution)/shard_map/ppermute | solution.py:482
  11.1 3.7 %collective-permute-start.4 = (f32[12,8,128]{2,1,0:T(8,128)S(1)}, f32[12,8,128]{2,1,0:T(8,128)S(1)}, u32[]{:S(2)}, u32[]{:S(2)}) collective-permute-start(f32[12,8,128]{2,1,0:T(8,128)S(1)} %get-tuple-element.43), channel_id=1, source_target_pairs={{0,12},{4,0},{8,4},{12,8},{1,13},{5,1},{9,5},{13,9},{2,14},{6,2},{... | collective-permute-start | bytes 147464 | tf_op jit(solution)/shard_map/ppermute | solution.py:522
  14.7 1.7 %collective-permute-done.4.refs_5_ = f32[12,8,128]{2,1,0:T(8,128)S(1)} collective-permute-done((f32[12,8,128]{2,1,0:T(8,128)S(1)}, f32[12,8,128]{2,1,0:T(8,128)S(1)}, u32[]{:S(2)}, u32[]{:S(2)}) %collective-permute-start.4) | collective-permute-done | bytes 49184 | tf_op jit(solution)/shard_map/ppermute | solution.py:522
  16.5 4.1 %collective-permute-done.3.refs_4_ = f32[12,8,128]{2,1,0:T(8,128)S(1)} collective-permute-done((f32[12,8,128]{2,1,0:T(8,128)S(1)}, f32[12,8,128]{2,1,0:T(8,128)S(1)}, u32[]{:S(2)}, u32[]{:S(2)}) %collective-permute-start.3) | collective-permute-done | bytes 49184 | tf_op jit(solution)/shard_map/ppermute | solution.py:521
  20.6 18.8 %step.1 = (f32[3,2,2,2,128]{4,3,2,1,0:T(2,128)}, f32[2,2,2,8,128]{4,3,2,1,0:T(8,128)S(1)}, f32[2,2,8,128]{3,2,1,0:T(8,128)S(1)}) custom-call(f32[2,2,2,8,128]{4,3,2,1,0:T(8,128)S(1)} %get-tuple-element.15.refs_0_, f32[2,2,8,128]{3,2,1,0:T(8,128)S(1)} %collective-permute-done.refs_1_, f32[2,2,2,8,128]{4,3,2,1,0:T(8,128)S(1)} %collective-permute-done.1.refs_2_, ...), custom_call_target="tpu_custom_call" | custom-call | tf_op jit(solution)/shard_map/step/pallas_call | solution.py:564
  39.5 0.7 collective-permute-start.5
  40.1 1.5 %collective-permute-start.6 = (f32[2,2,2,8,128]{4,3,2,1,0:T(8,128)S(1)}, f32[2,2,2,8,128]{4,3,2,1,0:T(8,128)S(1)}, u32[]{:S(2)}, u32[]{:S(2)}) collective-permute-start(f32[2,2,2,8,128]{4,3,2,1,0:T(8,128)S(1)} %get-tuple-element.18.refs_0_), channel_id=1, source_target_pairs={{0,2},{2,0},{1,3},{3,1},{4,6},{6,4},{5,7},{7,5},{8,10},{10,8},{9,1... | collective-permute-start | bytes 98312 | tf_op jit(solution)/shard_map/ppermute | solution.py:482
  41.6 2.4 %collective-permute-done.6.refs_2_ = f32[2,2,2,8,128]{4,3,2,1,0:T(8,128)S(1)} collective-permute-done((f32[2,2,2,8,128]{4,3,2,1,0:T(8,128)S(1)}, f32[2,2,2,8,128]{4,3,2,1,0:T(8,128)S(1)}, u32[]{:S(2)}, u32[]{:S(2)}) %collective-permute-start.6) | collective-permute-done | bytes 32800 | tf_op jit(solution)/shard_map/ppermute | solution.py:482
  44.1 0.1 collective-permute-start.9
  44.1 2.0 %collective-permute-start.8 = (f32[12,8,128]{2,1,0:T(8,128)S(1)}, f32[12,8,128]{2,1,0:T(8,128)S(1)}, u32[]{:S(2)}, u32[]{:S(2)}) collective-permute-start(f32[12,8,128]{2,1,0:T(8,128)S(1)} %get-tuple-element.38), channel_id=1, source_target_pairs={{0,4},{4,8},{8,12},{12,0},{1,5},{5,9},{9,13},{13,1},{2,6},{6,10},{... | collective-permute-start | bytes 147464 | tf_op jit(solution)/shard_map/ppermute | solution.py:521
  46.1 2.3 %collective-permute-done.9.refs_5_ = f32[12,8,128]{2,1,0:T(8,128)S(1)} collective-permute-done((f32[12,8,128]{2,1,0:T(8,128)S(1)}, f32[12,8,128]{2,1,0:T(8,128)S(1)}, u32[]{:S(2)}, u32[]{:S(2)}) %collective-permute-start.9) | collective-permute-done | bytes 49184 | tf_op jit(solution)/shard_map/ppermute | solution.py:522
  48.5 1.6 %collective-permute-done.8.refs_4_ = f32[12,8,128]{2,1,0:T(8,128)S(1)} collective-permute-done((f32[12,8,128]{2,1,0:T(8,128)S(1)}, f32[12,8,128]{2,1,0:T(8,128)S(1)}, u32[]{:S(2)}, u32[]{:S(2)}) %collective-permute-start.8) | collective-permute-done | bytes 49184 | tf_op jit(solution)/shard_map/ppermute | solution.py:521
  50.1 20.9 %field.1 = (f32[3,2,2,2,128]{4,3,2,1,0:T(2,128)}, f32[16,128]{1,0:T(8,128)S(1)}) custom-call(f32[2,2,2,8,128]{4,3,2,1,0:T(8,128)S(1)} %get-tuple-element.18.refs_0_, f32[2,2,8,128]{3,2,1,0:T(8,128)S(1)} %collective-permute-done.5.refs_1_, f32[2,2,2,8,128]{4,3,2,1,0:T(8,128)S(1)} %collective-permute-done.6.refs_2_, ...), custom_call_target="tpu_custom_call" | custom-call | tf_op jit(solution)/shard_map/field/pallas_call | solution.py:574
  71.0 1.5 %collective-permute-start.11 = (f32[16,128]{1,0:T(8,128)S(1)}, f32[16,128]{1,0:T(8,128)S(1)}, u32[]{:S(2)}, u32[]{:S(2)}) collective-permute-start(f32[16,128]{1,0:T(8,128)S(1)} %get-tuple-element.21), channel_id=1, source_target_pairs={{0,2},{1,3},{2,0},{3,1},{4,6},{5,7},{6,4},{7,5},{8,10},{9,11},{10,... | collective-permute-start | bytes 24584 | tf_op jit(solution)/shard_map/ppermute | solution.py:528
  72.5 0.3 collective-permute-start.10
  72.9 1.3 %collective-permute-done.12 = f32[16,128]{1,0:T(8,128)S(1)} collective-permute-done((f32[16,128]{1,0:T(8,128)S(1)}, f32[16,128]{1,0:T(8,128)S(1)}, u32[]{:S(2)}, u32[]{:S(2)}) %collective-permute-start.12) | collective-permute-done | bytes 8224 | tf_op jit(solution)/shard_map/ppermute | solution.py:528
  74.1 0.6 collective-permute-done.11
  74.7 0.2 collective-permute-start.15
  74.9 1.5 %collective-permute-start.14 = (f32[16,128]{1,0:T(8,128)S(1)}, f32[16,128]{1,0:T(8,128)S(1)}, u32[]{:S(2)}, u32[]{:S(2)}) collective-permute-start(f32[16,128]{1,0:T(8,128)S(1)} %add_add_fusion.refs_0_), channel_id=1, source_target_pairs={{0,8},{4,12},{8,0},{12,4},{1,9},{5,13},{9,1},{13,5},{2,10},{6,14},... | collective-permute-start | bytes 24584 | tf_op jit(solution)/shard_map/ppermute | solution.py:528
  76.4 2.8 %collective-permute-start.13 = (f32[16,128]{1,0:T(8,128)S(1)}, f32[16,128]{1,0:T(8,128)S(1)}, u32[]{:S(2)}, u32[]{:S(2)}) collective-permute-start(f32[16,128]{1,0:T(8,128)S(1)} %add_add_fusion.refs_0_), channel_id=1, source_target_pairs={{0,4},{4,0},{8,12},{12,8},{1,5},{5,1},{9,13},{13,9},{2,6},{6,2},{1... | collective-permute-start | bytes 24584 | tf_op jit(solution)/shard_map/ppermute | solution.py:528
  79.2 1.1 %collective-permute-done.15.refs_3_ = f32[16,128]{1,0:T(8,128)S(1)} collective-permute-done((f32[16,128]{1,0:T(8,128)S(1)}, f32[16,128]{1,0:T(8,128)S(1)}, u32[]{:S(2)}, u32[]{:S(2)}) %collective-permute-start.15) | collective-permute-done | bytes 8224 | tf_op jit(solution)/shard_map/ppermute | solution.py:528
  80.2 0.6 collective-permute-done.13.refs_1_
  80.8 1.5 %library.1 = (f32[2,2,2]{2,1,0:T(2,128)}, f32[48,48]{1,0:T(8,128)}, f32[1,48]{1,0:T(1,128)}) custom-call(f32[48]{0:T(128)S(1)} %copy-done.4, f32[16,128]{1,0:T(8,128)S(1)} %add_add_fusion.refs_0_, f32[16,128]{1,0:T(8,128)S(1)} %collective-permute-done.13.refs_1_, f32[16,128]{1,0:T(8,128)S(1)} %collective-permute-done.14.refs_2_, ...), custom_call_target="tpu_custom_call" | custom-call | tf_op jit(solution)/shard_map/library/pallas_call | solution.py:585
  (30 shorter events, 0.1 us)
Async XLA Ops:
  0.6 0.7 copy-start
  1.3 0.7 copy-start.1
  2.0 0.7 copy-start.2
  2.7 0.7 copy-start.3
  4.0 7.0 %collective-permute-start.2 = (f32[2,2,8,128]{3,2,1,0:T(8,128)S(1)}, f32[2,2,8,128]{3,2,1,0:T(8,128)S(1)}, u32[]{:S(2)}, u32[]{:S(2)}) collective-permute-start(f32[2,2,8,128]{3,2,1,0:T(8,128)S(1)} %get-tuple-element.16), channel_id=1, source_target_pairs={{0,3},{1,2},{2,1},{3,0},{4,7},{5,6},{6,5},{7,4},{8,11},{9,10},{10,... | collective-permute-start | bytes 49160 | tf_op jit(solution)/shard_map/ppermute | solution.py:483
  6.5 1.5 %collective-permute-start = (f32[2,2,8,128]{3,2,1,0:T(8,128)S(1)}, f32[2,2,8,128]{3,2,1,0:T(8,128)S(1)}, u32[]{:S(2)}, u32[]{:S(2)}) collective-permute-start(f32[2,2,8,128]{3,2,1,0:T(8,128)S(1)} %get-tuple-element.16), channel_id=1, source_target_pairs={{0,1},{1,0},{2,3},{3,2},{4,5},{5,4},{6,7},{7,6},{8,9},{9,8},{10,11... | collective-permute-start | bytes 49160 | tf_op jit(solution)/shard_map/ppermute | solution.py:480
  7.1 3.9 %collective-permute-start.1 = (f32[2,2,2,8,128]{4,3,2,1,0:T(8,128)S(1)}, f32[2,2,2,8,128]{4,3,2,1,0:T(8,128)S(1)}, u32[]{:S(2)}, u32[]{:S(2)}) collective-permute-start(f32[2,2,2,8,128]{4,3,2,1,0:T(8,128)S(1)} %get-tuple-element.15.refs_0_), channel_id=1, source_target_pairs={{0,2},{2,0},{1,3},{3,1},{4,6},{6,4},{5,7},{7,5},{8,10},{10,8},{9,1... | collective-permute-start | bytes 98312 | tf_op jit(solution)/shard_map/ppermute | solution.py:482
  11.1 5.4 %collective-permute-start.4 = (f32[12,8,128]{2,1,0:T(8,128)S(1)}, f32[12,8,128]{2,1,0:T(8,128)S(1)}, u32[]{:S(2)}, u32[]{:S(2)}) collective-permute-start(f32[12,8,128]{2,1,0:T(8,128)S(1)} %get-tuple-element.43), channel_id=1, source_target_pairs={{0,12},{4,0},{8,4},{12,8},{1,13},{5,1},{9,5},{13,9},{2,14},{6,2},{... | collective-permute-start | bytes 147464 | tf_op jit(solution)/shard_map/ppermute | solution.py:522
  14.7 5.9 %collective-permute-start.3 = (f32[12,8,128]{2,1,0:T(8,128)S(1)}, f32[12,8,128]{2,1,0:T(8,128)S(1)}, u32[]{:S(2)}, u32[]{:S(2)}) collective-permute-start(f32[12,8,128]{2,1,0:T(8,128)S(1)} %get-tuple-element.44), channel_id=1, source_target_pairs={{0,4},{4,8},{8,12},{12,0},{1,5},{5,9},{9,13},{13,1},{2,6},{6,10},{... | collective-permute-start | bytes 147464 | tf_op jit(solution)/shard_map/ppermute | solution.py:521
  39.5 4.6 %collective-permute-start.7 = (f32[2,2,8,128]{3,2,1,0:T(8,128)S(1)}, f32[2,2,8,128]{3,2,1,0:T(8,128)S(1)}, u32[]{:S(2)}, u32[]{:S(2)}) collective-permute-start(f32[2,2,8,128]{3,2,1,0:T(8,128)S(1)} %get-tuple-element.19), channel_id=1, source_target_pairs={{0,3},{1,2},{2,1},{3,0},{4,7},{5,6},{6,5},{7,4},{8,11},{9,10},{10,... | collective-permute-start | bytes 49160 | tf_op jit(solution)/shard_map/ppermute | solution.py:483
  39.5 2.2 %collective-permute-start.5 = (f32[2,2,8,128]{3,2,1,0:T(8,128)S(1)}, f32[2,2,8,128]{3,2,1,0:T(8,128)S(1)}, u32[]{:S(2)}, u32[]{:S(2)}) collective-permute-start(f32[2,2,8,128]{3,2,1,0:T(8,128)S(1)} %get-tuple-element.19), channel_id=1, source_target_pairs={{0,1},{1,0},{2,3},{3,2},{4,5},{5,4},{6,7},{7,6},{8,9},{9,8},{10,11... | collective-permute-start | bytes 49160 | tf_op jit(solution)/shard_map/ppermute | solution.py:480
  40.1 3.9 %collective-permute-start.6 = (f32[2,2,2,8,128]{4,3,2,1,0:T(8,128)S(1)}, f32[2,2,2,8,128]{4,3,2,1,0:T(8,128)S(1)}, u32[]{:S(2)}, u32[]{:S(2)}) collective-permute-start(f32[2,2,2,8,128]{4,3,2,1,0:T(8,128)S(1)} %get-tuple-element.18.refs_0_), channel_id=1, source_target_pairs={{0,2},{2,0},{1,3},{3,1},{4,6},{6,4},{5,7},{7,5},{8,10},{10,8},{9,1... | collective-permute-start | bytes 98312 | tf_op jit(solution)/shard_map/ppermute | solution.py:482
  44.1 4.4 %collective-permute-start.9 = (f32[12,8,128]{2,1,0:T(8,128)S(1)}, f32[12,8,128]{2,1,0:T(8,128)S(1)}, u32[]{:S(2)}, u32[]{:S(2)}) collective-permute-start(f32[12,8,128]{2,1,0:T(8,128)S(1)} %get-tuple-element.37), channel_id=1, source_target_pairs={{0,12},{4,0},{8,4},{12,8},{1,13},{5,1},{9,5},{13,9},{2,14},{6,2},{... | collective-permute-start | bytes 147464 | tf_op jit(solution)/shard_map/ppermute | solution.py:522
  44.1 5.9 %collective-permute-start.8 = (f32[12,8,128]{2,1,0:T(8,128)S(1)}, f32[12,8,128]{2,1,0:T(8,128)S(1)}, u32[]{:S(2)}, u32[]{:S(2)}) collective-permute-start(f32[12,8,128]{2,1,0:T(8,128)S(1)} %get-tuple-element.38), channel_id=1, source_target_pairs={{0,4},{4,8},{8,12},{12,0},{1,5},{5,9},{9,13},{13,1},{2,6},{6,10},{... | collective-permute-start | bytes 147464 | tf_op jit(solution)/shard_map/ppermute | solution.py:521
  71.0 9.8 %copy-start.4 = (f32[48]{0:T(128)S(1)}, f32[48]{0:T(128)}, u32[]{:S(2)}) copy-start(f32[48]{0:T(128)} %coefficients.1) | copy-start | bytes 580
  71.0 3.1 %collective-permute-start.12 = (f32[16,128]{1,0:T(8,128)S(1)}, f32[16,128]{1,0:T(8,128)S(1)}, u32[]{:S(2)}, u32[]{:S(2)}) collective-permute-start(f32[16,128]{1,0:T(8,128)S(1)} %get-tuple-element.21), channel_id=1, source_target_pairs={{0,3},{1,2},{2,1},{3,0},{4,7},{5,6},{6,5},{7,4},{8,11},{9,10},{10,... | collective-permute-start | bytes 24584 | tf_op jit(solution)/shard_map/ppermute | solution.py:528
  71.0 3.7 %collective-permute-start.11 = (f32[16,128]{1,0:T(8,128)S(1)}, f32[16,128]{1,0:T(8,128)S(1)}, u32[]{:S(2)}, u32[]{:S(2)}) collective-permute-start(f32[16,128]{1,0:T(8,128)S(1)} %get-tuple-element.21), channel_id=1, source_target_pairs={{0,2},{1,3},{2,0},{3,1},{4,6},{5,7},{6,4},{7,5},{8,10},{9,11},{10,... | collective-permute-start | bytes 24584 | tf_op jit(solution)/shard_map/ppermute | solution.py:528
  72.5 2.2 %collective-permute-start.10 = (f32[16,128]{1,0:T(8,128)S(1)}, f32[16,128]{1,0:T(8,128)S(1)}, u32[]{:S(2)}, u32[]{:S(2)}) collective-permute-start(f32[16,128]{1,0:T(8,128)S(1)} %get-tuple-element.21), channel_id=1, source_target_pairs={{0,1},{1,0},{2,3},{3,2},{4,5},{5,4},{6,7},{7,6},{8,9},{9,8},{10,11... | collective-permute-start | bytes 24584 | tf_op jit(solution)/shard_map/ppermute | solution.py:528
  74.7 5.5 %collective-permute-start.15 = (f32[16,128]{1,0:T(8,128)S(1)}, f32[16,128]{1,0:T(8,128)S(1)}, u32[]{:S(2)}, u32[]{:S(2)}) collective-permute-start(f32[16,128]{1,0:T(8,128)S(1)} %add_add_fusion.refs_0_), channel_id=1, source_target_pairs={{0,12},{4,8},{8,4},{12,0},{1,13},{5,9},{9,5},{13,1},{2,14},{6,10},... | collective-permute-start | bytes 24584 | tf_op jit(solution)/shard_map/ppermute | solution.py:528
  74.9 5.3 %collective-permute-start.14 = (f32[16,128]{1,0:T(8,128)S(1)}, f32[16,128]{1,0:T(8,128)S(1)}, u32[]{:S(2)}, u32[]{:S(2)}) collective-permute-start(f32[16,128]{1,0:T(8,128)S(1)} %add_add_fusion.refs_0_), channel_id=1, source_target_pairs={{0,8},{4,12},{8,0},{12,4},{1,9},{5,13},{9,1},{13,5},{2,10},{6,14},... | collective-permute-start | bytes 24584 | tf_op jit(solution)/shard_map/ppermute | solution.py:528
  76.4 4.4 %collective-permute-start.13 = (f32[16,128]{1,0:T(8,128)S(1)}, f32[16,128]{1,0:T(8,128)S(1)}, u32[]{:S(2)}, u32[]{:S(2)}) collective-permute-start(f32[16,128]{1,0:T(8,128)S(1)} %add_add_fusion.refs_0_), channel_id=1, source_target_pairs={{0,4},{4,0},{8,12},{12,8},{1,5},{5,1},{9,13},{13,9},{2,6},{6,2},{1... | collective-permute-start | bytes 24584 | tf_op jit(solution)/shard_map/ppermute | solution.py:528
